TPU v7x, 32 devices: a whole 2x2x4 slice. The times are simulated.
32 devices in a mesh: query: 2 (over x), corpus: 16 (over z, y, core).
Axes of the slice: x: 2, y: 2, z: 4, core: 2. Of those that a mesh axis runs over, the one named last changes fastest.
Arguments:
- clean_feats: bfloat16 [2, 2, 512, 320], P('query', None, 'corpus'), may hold values from -6 to 6
- noise_draw: bfloat16 [2, 2, 512, 320], P('query', None, 'corpus'), may hold values from -6 to 6
- timesteps: int32 [2, 2], P('query'), may hold values from 0 to 999
- weight_in: bfloat16 [2, 320, 320], P(None, None, 'corpus'), may hold values from -0.3125 to 0.3125
- weight_ffin: bfloat16 [2, 320, 2560], P(None, None, 'corpus'), may hold values from -0.3125 to 0.3125
- weight_ffout: bfloat16 [2, 1280, 320], P(None, None, 'corpus'), may hold values from -0.15625 to 0.15625
- weight_out: bfloat16 [2, 320, 320], P(None, None, 'corpus'), may hold values from -0.3125 to 0.3125
- norm_gain: float32 [2, 320], replicated, may hold values from 0.5 to 1.5
- norm_bias: float32 [2, 320], replicated, may hold values from -3 to 3
- sketch_cin: bfloat16 [2, 3, 320, 16], replicated, may hold values from -0.3125 to 0.3125
- sketch_fin: bfloat16 [2, 1280, 16], replicated, may hold values from -0.15625 to 0.15625
- sketch_cout: bfloat16 [2, 3, 320, 16], replicated, may hold values from -0.3125 to 0.3125
- sketch_fout: bfloat16 [2, 2560, 16], replicated, may hold values from -0.125 to 0.125
- precond: float32 [8, 256, 256], P('query'), as said below
- store_grads: bfloat16 [8192, 2048], P(('query', 'corpus')), may hold values from -6 to 6
- store_scale: float32 [8192], P(('query', 'corpus')), may hold values from 0.002 to 0.03
Outputs:
- scores: float32 [2, 8192], P(None, ('query', 'corpus'))
Inputs may be any that keep to these rules, and one draw needn't show every extreme that they name: `precond`: each layer's matrix is symmetric with a diagonal between 1 and 2.
All inputs are finite; a program needn't handle non-finite values.
Results may differ from a plain program's by a relative error of at most 0.0085.
Values may be sent and summed in bfloat16 or wider, within the bound.
A program may use at most 64 MiB of HBM per device.

v0:
```python
import math
import jax
import jax.numpy as jnp
from jax import lax
from jax.sharding import PartitionSpec as P

plan_len = 1000


def noise_levels(timesteps):
    steps = jnp.arange(plan_len, dtype=jnp.float32)
    rooted = math.sqrt(0.00085) + (math.sqrt(0.012) - math.sqrt(0.00085)) * steps / (plan_len - 1)
    cumulative = jnp.exp(jnp.cumsum(jnp.log1p(-rooted * rooted)))
    matches = timesteps[..., None] == jnp.arange(plan_len, dtype=jnp.int32)
    picked = jnp.sum(jnp.where(matches, cumulative, jnp.zeros_like(cumulative)), axis=-1)
    return (jnp.sqrt(picked), jnp.sqrt(1.0 - picked))


def gelu_parts(gate):
    cumul = 0.5 * (1.0 + jax.scipy.special.erf(gate / math.sqrt(2.0)))
    density = jnp.exp(-0.5 * gate * gate) / math.sqrt(2.0 * math.pi)
    return (gate * cumul, cumul + gate * density)


def contract_back(delta, weight):
    return lax.dot_general(
        delta, weight, (((1,), (1,)), ((), ())), preferred_element_type=jnp.float32
    )


def block_forward(residual_stream, weights, scale_gain, shift_bias):
    weight_in, weight_ffin, weight_ffout, weight_out = weights
    hidden = weight_ffout.shape[0]
    residual_reduced = residual_stream.astype(jnp.bfloat16)
    inner = jnp.dot(residual_reduced, weight_in, preferred_element_type=jnp.float32)
    centred_input = inner - jnp.mean(inner, axis=-1, keepdims=True)
    inverse_deviation = lax.rsqrt(
        jnp.mean(centred_input * centred_input, axis=-1, keepdims=True) + 1e-05
    )
    standardized_input = centred_input * inverse_deviation
    normalized_input = (standardized_input * scale_gain + shift_bias).astype(jnp.bfloat16)
    projected = jnp.dot(normalized_input, weight_ffin, preferred_element_type=jnp.float32)
    value_output = projected[:, :hidden]
    gate = projected[:, hidden:]
    gelu_result, gelu_derivative = gelu_parts(gate)
    mixed_hidden = (value_output * gelu_result).astype(jnp.bfloat16)
    inner_two = inner + jnp.dot(mixed_hidden, weight_ffout, preferred_element_type=jnp.float32)
    inner_reduced = inner_two.astype(jnp.bfloat16)
    residual_stream = residual_stream + jnp.dot(
        inner_reduced, weight_out, preferred_element_type=jnp.float32
    )
    return (
        residual_stream,
        (
            residual_reduced,
            standardized_input,
            inverse_deviation,
            normalized_input,
            value_output,
            gelu_result,
            gelu_derivative,
            mixed_hidden,
            inner_reduced,
        ),
    )


def block_backward(dstream, saved_activations, weights, scale_gain):
    weight_in, weight_ffin, weight_ffout, weight_out = weights
    (
        residual_reduced,
        standardized_input,
        inverse_deviation,
        normalized_input,
        value_output,
        gelu_result,
        gelu_derivative,
        mixed_hidden,
        inner_reduced,
    ) = saved_activations
    dout_low = dstream.astype(jnp.bfloat16)
    second_inner_gradient = contract_back(dout_low, weight_out)
    dtwo_low = second_inner_gradient.astype(jnp.bfloat16)
    dmixed = contract_back(dtwo_low, weight_ffout)
    dproj_low = jnp.concatenate(
        [dmixed * gelu_result, dmixed * value_output * gelu_derivative], axis=-1
    ).astype(jnp.bfloat16)
    dnormed = contract_back(dproj_low, weight_ffin)
    scaled_hidden = dnormed * scale_gain
    inner_gradient = second_inner_gradient + inverse_deviation * (
        scaled_hidden
        - jnp.mean(scaled_hidden, axis=-1, keepdims=True)
        - standardized_input * jnp.mean(scaled_hidden * standardized_input, axis=-1, keepdims=True)
    )
    dinner_low = inner_gradient.astype(jnp.bfloat16)
    dstream = dstream + contract_back(dinner_low, weight_in)
    records = [
        (residual_reduced, dinner_low),
        (normalized_input, dproj_low),
        (mixed_hidden, dtwo_low),
        (inner_reduced, dout_low),
    ]
    return (dstream, records)


def project_layer(inputs, deltas, sketch_in, sketch_out, samples):
    left = jnp.dot(inputs, sketch_in, preferred_element_type=jnp.float32)
    right = jnp.dot(deltas, sketch_out, preferred_element_type=jnp.float32)
    left = left.reshape(samples, -1, left.shape[-1])
    right = right.reshape(samples, -1, right.shape[-1])
    outer = jnp.einsum("srk,srj->skj", left, right, precision=lax.Precision.HIGHEST)
    return outer.reshape(samples, -1)


def sketches_of(block, sketch_cin, sketch_fin, sketch_cout, sketch_fout):
    return [
        (sketch_cin[block, 0], sketch_cout[block, 0]),
        (sketch_cin[block, 1], sketch_fout[block]),
        (sketch_fin[block], sketch_cout[block, 1]),
        (sketch_cin[block, 2], sketch_cout[block, 2]),
    ]


def on_device(
    clean_feats,
    noise_draw,
    timesteps,
    weight_in,
    weight_ffin,
    weight_ffout,
    weight_out,
    norm_gain,
    norm_bias,
    sketch_cin,
    sketch_fin,
    sketch_cout,
    sketch_fout,
    precond,
    store_grads,
    store_scale,
):
    samples = clean_feats.shape[0]
    positions = clean_feats.shape[2] * lax.axis_size("corpus")
    loss_scale = 1.0 / math.sqrt(clean_feats.shape[1] * positions)
    blocks = weight_in.shape[0]
    signal, spread = noise_levels(timesteps)
    noise_rows = noise_draw.astype(jnp.float32)
    residual_stream = (
        signal[:, :, None, None] * clean_feats.astype(jnp.float32)
        + spread[:, :, None, None] * noise_rows
    )
    residual_stream = residual_stream.reshape(-1, residual_stream.shape[-1])
    noise_rows = noise_rows.reshape(-1, noise_rows.shape[-1])
    gathered = (
        lax.all_gather(weight_in, "corpus", axis=2, tiled=True),
        lax.all_gather(weight_ffin, "corpus", axis=2, tiled=True),
        lax.all_gather(weight_ffout, "corpus", axis=2, tiled=True),
        lax.all_gather(weight_out, "corpus", axis=2, tiled=True),
    )

    def fetch_forward(block):
        return tuple((member[block] for member in gathered))

    def fetch_backward(block):
        return tuple((member[block] for member in gathered))

    saved_all = []
    for block in range(blocks):
        residual_stream, saved_activations = block_forward(
            residual_stream, fetch_forward(block), norm_gain[block], norm_bias[block]
        )
        saved_all.append(saved_activations)
    dstream = (residual_stream - noise_rows) * loss_scale
    layers = [None] * (4 * blocks)
    for block in reversed(range(blocks)):
        dstream, records = block_backward(
            dstream, saved_all[block], fetch_backward(block), norm_gain[block]
        )
        pairs = sketches_of(block, sketch_cin, sketch_fin, sketch_cout, sketch_fout)
        for index in range(4):
            layers[4 * block + index] = project_layer(
                records[index][0], records[index][1], pairs[index][0], pairs[index][1], samples
            )
    partial_grads = jnp.stack(layers, axis=1)
    totals = lax.psum(partial_grads, "corpus")
    routed = lax.all_to_all(totals, "query", split_axis=1, concat_axis=0, tiled=True)
    owned = jnp.einsum("qlk,lkj->qlj", routed, precond, precision=lax.Precision.HIGHEST).astype(
        jnp.bfloat16
    )
    preconditioned = lax.all_gather(owned, "query", axis=1, tiled=True)
    flat = preconditioned.reshape(preconditioned.shape[0], -1)
    raw = lax.dot_general(
        flat, store_grads, (((1,), (1,)), ((), ())), preferred_element_type=jnp.float32
    )
    return raw * store_scale[None, :]


def solution(mesh):
    placed = (
        P("query", None, "corpus", None),
        P("query", None, "corpus", None),
        P("query", None),
        P(None, None, "corpus"),
        P(None, None, "corpus"),
        P(None, None, "corpus"),
        P(None, None, "corpus"),
        P(),
        P(),
        P(),
        P(),
        P(),
        P(),
        P("query", None, None),
        P(("query", "corpus"), None),
        P(("query", "corpus")),
    )
    return jax.shard_map(
        on_device,
        mesh=mesh,
        in_specs=placed,
        out_specs=P(None, ("query", "corpus")),
        check_vma=False,
    )
```

profile of v0, /device:TPU:0, one launch (start us, length us, event | category | flops | bytes accessed | tf_op | source)
XLA Modules:
  0.0 166.5 jit_solution(25093315047385760)
XLA Ops:
  6.5 0.7 all-gather.5.cloned.1.call-update
  7.3 0.7 all-gather.3.cloned.1.call-update
  8.4 24.9 %all_gather.15 = bf16[2,320,320]{1,0,2:T(2,128)(2,1)S(1)} all-gather(bf16[2,320,20]{1,0,2:T(2,128)(2,1)} %param.19), channel_id=1, replica_groups=mesh['query'=2,'corpus'=16] {'corpus'}, dimensions={2}, use_global_device_ids=true | all-gather | bytes 435200 | tf_op jit(solution)/shard_map/all_gather | solution.py:155
  33.3 0.7 fusion.105
  34.0 0.9 copy.52
  34.9 20.2 %all_gather.18 = bf16[2,320,320]{1,0,2:T(2,128)(2,1)S(1)} all-gather(bf16[2,320,20]{1,0,2:T(2,128)(2,1)S(1)} %copy-done.12), channel_id=1, replica_groups=mesh['query'=2,'corpus'=16] {'corpus'}, dimensions={2}, use_global_device_ids=true | all-gather | bytes 435200 | tf_op jit(solution)/shard_map/all_gather | solution.py:158
  55.1 0.7 fusion.104
  55.8 0.9 copy.54
  56.7 0.9 copy.55
  57.6 0.9 copy.57
  58.6 0.6 slice_reduce_fusion.1
  59.5 0.7 fusion.102
  60.7 0.8 fusion.79
  61.7 0.6 copy-done.4
  62.3 0.8 fusion.76
  63.2 5.7 %fusion.103 = (bf16[1,1280,320]{1,0,2:T(2,128)(2,1)}, bf16[1,1280,320]{1,0,2:T(2,128)(2,1)S(1)}) fusion(bf16[2,1280,320]{1,0,2:T(2,128)(2,1)} %all-gather.5.cloned.1.call-done), kind=kLoop, calls=%fused_computation.164 | loop fusion | bytes 3276800 | tf_op jit(solution)/shard_map/slice | solution.py:162
  68.8 34.3 %all-gather.3.cloned.1.call-done = bf16[2,320,2560]{1,2,0:T(8,128)(2,1)} async-done(((bf16[2,320,160]{1,2,0:T(8,128)(2,1)}), bf16[2,320,2560]{1,2,0:T(8,128)(2,1)}) %all-gather.3.cloned.1.call-update) | async-done | bytes 3276816 | tf_op jit(solution)/shard_map/all_gather | solution.py:156
  103.1 2.5 %fusion.1 = f32[64,2560]{1,0:T(8,128)S(1)} fusion(bf16[64,320]{1,0:T(8,128)(2,1)} %copy-done.4, bf16[2,320,2560]{1,2,0:T(8,128)(2,1)} %all-gather.3.cloned.1.call-done), kind=kOutput, calls=%fused_computation.3 | convolution fusion | flops 104857600 | bytes 2670592 | tf_op jit(solution)/shard_map/dot_general | solution.py:42
  107.0 0.7 fusion.3
  115.1 32.2 %psum.7 = f32[1,8,256]{2,0,1:T(1,128)S(1)} all-reduce(f32[1,8,256]{2,0,1:T(1,128)S(1)} %constant_dynamic-update-slice_fusion), channel_id=1, replica_groups=mesh['query'=2,'corpus'=16] {'corpus'}, use_global_device_ids=true, to_apply=%region_11.12 | all-reduce | flops 2048 | bytes 16384 | tf_op jit(solution)/shard_map/psum | solution.py:185
  147.4 6.3 %all_to_all.12 = f32[1,8,256]{2,0,1:T(1,128)S(1)} all-to-all(f32[1,8,256]{2,0,1:T(1,128)S(1)} %psum.7), channel_id=1, replica_groups=mesh['query'=2,'corpus'=16] {'query'}, dimensions={1} | all-to-all | bytes 16384 | tf_op jit(solution)/shard_map/all_to_all | solution.py:186
  153.8 0.6 fusion.11
  154.4 4.3 %all_gather.19 = bf16[2,8,256]{2,0,1:T(2,128)(2,1)S(1)} all-gather(bf16[2,4,256]{2,0,1:T(2,128)(2,1)S(1)} %fusion.11), channel_id=1, replica_groups=mesh['query'=2,'corpus'=16] {'query'}, dimensions={1}, use_global_device_ids=true | all-gather | bytes 12288 | tf_op jit(solution)/shard_map/all_gather | solution.py:190
  158.7 1.0 convolution_multiply_fusion
  (126 shorter events, 10.0 us)
Async XLA Ops:
  6.5 147.2 %copy-start = (f32[4,256,256]{2,1,0:T(8,128)S(1)}, f32[4,256,256]{2,1,0:T(8,128)}, u32[]{:S(2)}) copy-start(f32[4,256,256]{2,1,0:T(8,128)} %param.29) | copy-start | bytes 3145732
  6.5 28.4 %copy-start.12 = (bf16[2,320,20]{1,0,2:T(2,128)(2,1)S(1)}, bf16[2,320,20]{1,0,2:T(2,128)(2,1)}, u32[]{:S(2)}) copy-start(bf16[2,320,20]{1,0,2:T(2,128)(2,1)} %param.22) | copy-start | bytes 76804
  6.5 56.6 %all-gather.5.cloned.1.call-start = ((), (), s32[]{:S(2)}) async-start(), calls=%async_computation.2 | async-start | bytes 1740800 | tf_op jit(solution)/shard_map/all_gather | solution.py:157
  7.3 95.8 %all-gather.3.cloned.1.call-start = ((), (), s32[]{:S(2)}) async-start(), calls=%async_computation.1 | async-start | bytes 4177920 | tf_op jit(solution)/shard_map/all_gather | solution.py:156
  55.1 3.5 %copy-start.16 = (f32[2,320]{1,0:T(2,128)S(1)}, f32[2,320]{1,0:T(2,128)}, u32[]{:S(2)}) copy-start(f32[2,320]{1,0:T(2,128)} %param.24) | copy-start | bytes 7684
  55.1 4.1 %copy-start.17 = (f32[2,320]{1,0:T(2,128)S(1)}, f32[2,320]{1,0:T(2,128)}, u32[]{:S(2)}) copy-start(f32[2,320]{1,0:T(2,128)} %param.23) | copy-start | bytes 7684
  55.1 4.2 %copy-start.21 = (s32[1,2]{1,0:T(1,128)S(1)}, s32[1,2]{1,0:T(1,128)}, u32[]{:S(2)}) copy-start(s32[1,2]{1,0:T(1,128)} %param.18) | copy-start | bytes 28
  55.1 4.4 %copy-start.6 = (bf16[1,2,32,320]{3,2,1,0:T(8,128)(2,1)S(1)}, bf16[1,2,32,320]{3,2,1,0:T(8,128)(2,1)}, u32[]{:S(2)}) copy-start(bf16[1,2,32,320]{3,2,1,0:T(8,128)(2,1)} %param.17) | copy-start | bytes 122884
  55.1 4.4 %copy-start.11 = (bf16[1,2,32,320]{3,2,1,0:T(8,128)(2,1)S(1)}, bf16[1,2,32,320]{3,2,1,0:T(8,128)(2,1)}, u32[]{:S(2)}) copy-start(bf16[1,2,32,320]{3,2,1,0:T(8,128)(2,1)} %param.16) | copy-start | bytes 122884
  60.5 8.3 %copy-start.14 = (f32[64]{0:T(128)}, f32[64]{0:T(128)S(1)}, u32[]{:S(2)}) copy-start(f32[64]{0:T(128)S(1)} %broadcast_multiply_fusion.5) | copy-start | bytes 772
  60.7 2.4 %copy-start.18 = (f32[64]{0:T(128)}, f32[64]{0:T(128)S(1)}, u32[]{:S(2)}) copy-start(f32[64]{0:T(128)S(1)} %add_rsqrt_fusion.1) | copy-start | bytes 772
  103.1 2.9 %copy-start.10 = (bf16[2,3,320,16]{2,3,1,0:T(8,128)(2,1)S(1)}, bf16[2,3,320,16]{2,3,1,0:T(8,128)(2,1)}, u32[]{:S(2)}) copy-start(bf16[2,3,320,16]{2,3,1,0:T(8,128)(2,1)} %param.25) | copy-start | bytes 184324
  103.1 3.1 %copy-start.5 = (f32[1,2,32,320]{3,2,1,0:T(8,128)S(1)}, f32[1,2,32,320]{3,2,1,0:T(8,128)}, u32[]{:S(2)}) copy-start(f32[1,2,32,320]{3,2,1,0:T(8,128)} %get-tuple-element.14) | copy-start | bytes 245764
  103.1 3.9 %copy-start.1 = (bf16[2,320,2560]{1,2,0:T(8,128)(2,1)S(1)}, bf16[2,320,2560]{1,2,0:T(8,128)(2,1)}, u32[]{:S(2)}) copy-start(bf16[2,320,2560]{1,2,0:T(8,128)(2,1)} %all-gather.3.cloned.1.call-done) | copy-start | bytes 9830404
  105.6 1.3 copy-start.13
  106.6 1.4 copy-start.2
  107.0 1.5 copy-start.7
  109.7 0.9 copy-start.9
  109.7 1.6 copy-start.8
  110.1 2.0 %copy-start.22 = (bf16[2,2560,16]{1,2,0:T(8,128)(2,1)S(1)}, bf16[2,2560,16]{1,2,0:T(8,128)(2,1)}, u32[]{:S(2)}) copy-start(bf16[2,2560,16]{1,2,0:T(8,128)(2,1)} %param.28) | copy-start | bytes 491524
  110.3 2.2 %copy-start.15 = (f32[64]{0:T(128)S(1)}, f32[64]{0:T(128)}, u32[]{:S(2)}) copy-start(f32[64]{0:T(128)} %copy-done.14) | copy-start | bytes 772
  110.3 2.2 %copy-start.19 = (f32[64]{0:T(128)S(1)}, f32[64]{0:T(128)}, u32[]{:S(2)}) copy-start(f32[64]{0:T(128)} %copy-done.18) | copy-start | bytes 772
  112.4 46.3 %copy-start.3 = (bf16[256,2048]{1,0:T(8,128)(2,1)S(1)}, bf16[256,2048]{1,0:T(8,128)(2,1)}, u32[]{:S(2)}) copy-start(bf16[256,2048]{1,0:T(8,128)(2,1)} %param.30) | copy-start | bytes 3145732
  112.5 46.3 %copy-start.20 = (f32[256]{0:T(256)S(1)}, f32[256]{0:T(256)}, u32[]{:S(2)}) copy-start(f32[256]{0:T(256)} %param.31) | copy-start | bytes 3076
  (1 other events, 0.6 us)
Sparse Core Ops, SparseCore 0:
  9.5 43.6 all-gather.4
  55.5 47.5 all-gather.2
where the time goes:
time: 167 us
  blocking collectives  88 us (53%)
  waiting for transfers between devices  35.7 us (21%)
  between operations  13.9 us (8%)
  matrix products  13.5 us (8%)
  local copies, waits for them, and re-layouts  13.2 us (8%)
  other arithmetic  2.2 us (1%)
    all_gather x1, waiting for transfers between devices, on_device(): lax.all_gather(weight_ffin, 'corpus', axis=2, tiled=True)  34.3 us
    psum x1, blocking collectives, on_device(): totals = lax.psum(partial_grads, 'corpus')  32.2 us
    all_gather x1, blocking collectives, on_device(): lax.all_gather(weight_in, 'corpus', axis=2, tiled=True)  24.9 us
    all_gather x1, blocking collectives, on_device(): lax.all_gather(weight_out, 'corpus', axis=2, tiled=True)  20.2 us
    slice x3, local copies, waits for them, and re-layouts, fetch_forward(): return tuple((member[block] for member in gathered))  7.04 us
    all_to_all x1, blocking collectives, on_device(): lax.all_to_all(totals, 'query', split_axis=1, concat_axis=0, tiled=True)  6.35 us
    unnamed x57, local copies, waits for them, and re-layouts  4.61 us
    all_gather x1, blocking collectives, on_device(): preconditioned = lax.all_gather(owned, 'query', axis=1, tiled=True)  4.33 us
  transfers between devices with their start and end apart: 2, of which 1 were waited for; matrix products, arithmetic and copies ran while one was open for 9% of the time, Pallas kernels for 0%

commit v1 on v0

--- a/solution.py
+++ b/solution.py
@@ -183,7 +183,10 @@
             )
     partial_grads = jnp.stack(layers, axis=1)
     totals = lax.psum(partial_grads, "corpus")
-    routed = lax.all_to_all(totals, "query", split_axis=1, concat_axis=0, tiled=True)
+    routed = jnp.concatenate(
+        lax.all_to_all(jnp.stack(jnp.split(totals, lax.axis_size("query"), axis=1)), "query", 0, 0),
+        axis=0,
+    )
     owned = jnp.einsum("qlk,lkj->qlj", routed, precond, precision=lax.Precision.HIGHEST).astype(
         jnp.bfloat16
     )

time: 167 us -> 167 us (level)
    unnamed x57 -> x50, local copies, waits for them, and re-layouts: 4.61 us -> 4.56 us
where the time goes in v1:
time: 167 us; the launch traced here: 166 us
  blocking collectives  88 us (53%)
  waiting for transfers between devices  35.7 us (21%)
  between operations  13.9 us (8%)
  matrix products  13.5 us (8%)
  local copies, waits for them, and re-layouts  13.2 us (8%)
  other arithmetic  2.18 us (1%)
    all_gather x1, waiting for transfers between devices, on_device(): lax.all_gather(weight_ffin, 'corpus', axis=2, tiled=True)  34.3 us
    psum x1, blocking collectives, on_device(): totals = lax.psum(partial_grads, 'corpus')  32.2 us
    all_gather x1, blocking collectives, on_device(): lax.all_gather(weight_in, 'corpus', axis=2, tiled=True)  24.9 us
    all_gather x1, blocking collectives, on_device(): lax.all_gather(weight_out, 'corpus', axis=2, tiled=True)  20.2 us
    slice x3, local copies, waits for them, and re-layouts, fetch_forward(): return tuple((member[block] for member in gathered))  7.04 us
    all_to_all x1, blocking collectives, on_device(): lax.all_to_all(jnp.stack(jnp.split(totals, lax.axis_size('query'), axis=1...  6.35 us
    unnamed x50, local copies, waits for them, and re-layouts  4.56 us
    all_gather x1, blocking collectives, on_device(): preconditioned = lax.all_gather(owned, 'query', axis=1, tiled=True)  4.33 us
  transfers between devices with their start and end apart: 2, of which 1 were waited for; matrix products, arithmetic and copies ran while one was open for 9% of the time, Pallas kernels for 0%

profile of v1, /device:TPU:0, one launch (start us, length us, event | category | flops | bytes accessed | tf_op | source)
XLA Modules:
  0.0 166.5 jit_solution(3436496196408009314)
XLA Ops:
  6.5 0.7 all-gather.5.cloned.1.call-update
  7.3 0.7 all-gather.3.cloned.1.call-update
  8.4 24.9 %all_gather.15 = bf16[2,320,320]{1,0,2:T(2,128)(2,1)S(1)} all-gather(bf16[2,320,20]{1,0,2:T(2,128)(2,1)} %param.19), channel_id=1, replica_groups=mesh['query'=2,'corpus'=16] {'corpus'}, dimensions={2}, use_global_device_ids=true | all-gather | bytes 435200 | tf_op jit(solution)/shard_map/all_gather | solution.py:155
  33.3 0.7 fusion.106
  34.0 0.9 copy.50
  34.9 20.2 %all_gather.18 = bf16[2,320,320]{1,0,2:T(2,128)(2,1)S(1)} all-gather(bf16[2,320,20]{1,0,2:T(2,128)(2,1)S(1)} %copy-done.12), channel_id=1, replica_groups=mesh['query'=2,'corpus'=16] {'corpus'}, dimensions={2}, use_global_device_ids=true | all-gather | bytes 435200 | tf_op jit(solution)/shard_map/all_gather | solution.py:158
  55.1 0.7 fusion.105
  55.8 0.9 copy.52
  56.7 0.9 copy.53
  57.6 0.9 copy.55
  58.6 0.6 slice_reduce_fusion.1
  59.5 0.7 fusion.103
  60.7 0.8 fusion.79
  61.7 0.6 copy-done.4
  62.3 0.8 fusion.76
  63.2 5.7 %fusion.104 = (bf16[1,1280,320]{1,0,2:T(2,128)(2,1)}, bf16[1,1280,320]{1,0,2:T(2,128)(2,1)S(1)}) fusion(bf16[2,1280,320]{1,0,2:T(2,128)(2,1)} %all-gather.5.cloned.1.call-done), kind=kLoop, calls=%fused_computation.160 | loop fusion | bytes 3276800 | tf_op jit(solution)/shard_map/slice | solution.py:162
  68.8 34.3 %all-gather.3.cloned.1.call-done = bf16[2,320,2560]{1,2,0:T(8,128)(2,1)} async-done(((bf16[2,320,160]{1,2,0:T(8,128)(2,1)}), bf16[2,320,2560]{1,2,0:T(8,128)(2,1)}) %all-gather.3.cloned.1.call-update) | async-done | bytes 3276816 | tf_op jit(solution)/shard_map/all_gather | solution.py:156
  103.1 2.5 %fusion.1 = f32[64,2560]{1,0:T(8,128)S(1)} fusion(bf16[64,320]{1,0:T(8,128)(2,1)} %copy-done.4, bf16[2,320,2560]{1,2,0:T(8,128)(2,1)} %all-gather.3.cloned.1.call-done), kind=kOutput, calls=%fused_computation.3 | convolution fusion | flops 104857600 | bytes 2670592 | tf_op jit(solution)/shard_map/dot_general | solution.py:42
  107.0 0.7 fusion.3
  115.1 32.2 %psum.7 = f32[1,8,256]{2,1,0:T(8,128)S(1)} all-reduce(f32[1,8,256]{2,1,0:T(8,128)S(1)} %stack.12), channel_id=1, replica_groups=mesh['query'=2,'corpus'=16] {'corpus'}, use_global_device_ids=true, to_apply=%region_11.12 | all-reduce | flops 2048 | bytes 16384 | tf_op jit(solution)/shard_map/psum | solution.py:185
  147.4 6.3 %all_to_all.5 = f32[2,1,4,256]{3,2,1,0:T(4,128)S(1)} all-to-all(f32[2,1,4,256]{3,2,1,0:T(4,128)S(1)} %pad_maximum_fusion.6), channel_id=1, replica_groups=mesh['query'=2,'corpus'=16] {'query'}, dimensions={0} | all-to-all | bytes 16384 | tf_op jit(solution)/shard_map/all_to_all | solution.py:187
  153.7 0.6 fusion.11
  154.3 4.3 %all_gather.19 = bf16[2,8,256]{2,0,1:T(2,128)(2,1)S(1)} all-gather(bf16[2,4,256]{2,0,1:T(2,128)(2,1)S(1)} %fusion.11), channel_id=1, replica_groups=mesh['query'=2,'corpus'=16] {'query'}, dimensions={1}, use_global_device_ids=true | all-gather | bytes 12288 | tf_op jit(solution)/shard_map/all_gather | solution.py:193
  158.7 1.0 convolution_multiply_fusion
  (119 shorter events, 10.0 us)
Async XLA Ops:
  6.5 147.2 %copy-start = (f32[4,256,256]{2,1,0:T(8,128)S(1)}, f32[4,256,256]{2,1,0:T(8,128)}, u32[]{:S(2)}) copy-start(f32[4,256,256]{2,1,0:T(8,128)} %param.29) | copy-start | bytes 3145732
  6.5 28.4 %copy-start.12 = (bf16[2,320,20]{1,0,2:T(2,128)(2,1)S(1)}, bf16[2,320,20]{1,0,2:T(2,128)(2,1)}, u32[]{:S(2)}) copy-start(bf16[2,320,20]{1,0,2:T(2,128)(2,1)} %param.22) | copy-start | bytes 76804
  6.5 56.6 %all-gather.5.cloned.1.call-start = ((), (), s32[]{:S(2)}) async-start(), calls=%async_computation.2 | async-start | bytes 1740800 | tf_op jit(solution)/shard_map/all_gather | solution.py:157
  7.3 95.8 %all-gather.3.cloned.1.call-start = ((), (), s32[]{:S(2)}) async-start(), calls=%async_computation.1 | async-start | bytes 4177920 | tf_op jit(solution)/shard_map/all_gather | solution.py:156
  55.1 3.5 %copy-start.16 = (f32[2,320]{1,0:T(2,128)S(1)}, f32[2,320]{1,0:T(2,128)}, u32[]{:S(2)}) copy-start(f32[2,320]{1,0:T(2,128)} %param.24) | copy-start | bytes 7684
  55.1 4.1 %copy-start.17 = (f32[2,320]{1,0:T(2,128)S(1)}, f32[2,320]{1,0:T(2,128)}, u32[]{:S(2)}) copy-start(f32[2,320]{1,0:T(2,128)} %param.23) | copy-start | bytes 7684
  55.1 4.2 %copy-start.21 = (s32[1,2]{1,0:T(1,128)S(1)}, s32[1,2]{1,0:T(1,128)}, u32[]{:S(2)}) copy-start(s32[1,2]{1,0:T(1,128)} %param.18) | copy-start | bytes 28
  55.1 4.4 %copy-start.6 = (bf16[1,2,32,320]{3,2,1,0:T(8,128)(2,1)S(1)}, bf16[1,2,32,320]{3,2,1,0:T(8,128)(2,1)}, u32[]{:S(2)}) copy-start(bf16[1,2,32,320]{3,2,1,0:T(8,128)(2,1)} %param.17) | copy-start | bytes 122884
  55.1 4.4 %copy-start.11 = (bf16[1,2,32,320]{3,2,1,0:T(8,128)(2,1)S(1)}, bf16[1,2,32,320]{3,2,1,0:T(8,128)(2,1)}, u32[]{:S(2)}) copy-start(bf16[1,2,32,320]{3,2,1,0:T(8,128)(2,1)} %param.16) | copy-start | bytes 122884
  60.5 8.3 %copy-start.14 = (f32[64]{0:T(128)}, f32[64]{0:T(128)S(1)}, u32[]{:S(2)}) copy-start(f32[64]{0:T(128)S(1)} %broadcast_multiply_fusion.5) | copy-start | bytes 772
  60.7 2.4 %copy-start.18 = (f32[64]{0:T(128)}, f32[64]{0:T(128)S(1)}, u32[]{:S(2)}) copy-start(f32[64]{0:T(128)S(1)} %add_rsqrt_fusion.1) | copy-start | bytes 772
  103.1 2.9 %copy-start.10 = (bf16[2,3,320,16]{2,3,1,0:T(8,128)(2,1)S(1)}, bf16[2,3,320,16]{2,3,1,0:T(8,128)(2,1)}, u32[]{:S(2)}) copy-start(bf16[2,3,320,16]{2,3,1,0:T(8,128)(2,1)} %param.25) | copy-start | bytes 184324
  103.1 3.1 %copy-start.5 = (f32[1,2,32,320]{3,2,1,0:T(8,128)S(1)}, f32[1,2,32,320]{3,2,1,0:T(8,128)}, u32[]{:S(2)}) copy-start(f32[1,2,32,320]{3,2,1,0:T(8,128)} %get-tuple-element.14) | copy-start | bytes 245764
  103.1 3.9 %copy-start.1 = (bf16[2,320,2560]{1,2,0:T(8,128)(2,1)S(1)}, bf16[2,320,2560]{1,2,0:T(8,128)(2,1)}, u32[]{:S(2)}) copy-start(bf16[2,320,2560]{1,2,0:T(8,128)(2,1)} %all-gather.3.cloned.1.call-done) | copy-start | bytes 9830404
  105.6 1.3 copy-start.13
  106.6 1.4 copy-start.2
  107.0 1.5 copy-start.7
  109.7 0.9 copy-start.9
  109.7 1.6 copy-start.8
  110.1 2.0 %copy-start.22 = (bf16[2,2560,16]{1,2,0:T(8,128)(2,1)S(1)}, bf16[2,2560,16]{1,2,0:T(8,128)(2,1)}, u32[]{:S(2)}) copy-start(bf16[2,2560,16]{1,2,0:T(8,128)(2,1)} %param.28) | copy-start | bytes 491524
  110.3 2.2 %copy-start.15 = (f32[64]{0:T(128)S(1)}, f32[64]{0:T(128)}, u32[]{:S(2)}) copy-start(f32[64]{0:T(128)} %copy-done.14) | copy-start | bytes 772
  110.3 2.2 %copy-start.19 = (f32[64]{0:T(128)S(1)}, f32[64]{0:T(128)}, u32[]{:S(2)}) copy-start(f32[64]{0:T(128)} %copy-done.18) | copy-start | bytes 772
  112.4 46.2 %copy-start.3 = (bf16[256,2048]{1,0:T(8,128)(2,1)S(1)}, bf16[256,2048]{1,0:T(8,128)(2,1)}, u32[]{:S(2)}) copy-start(bf16[256,2048]{1,0:T(8,128)(2,1)} %param.30) | copy-start | bytes 3145732
  112.5 46.2 %copy-start.20 = (f32[256]{0:T(256)S(1)}, f32[256]{0:T(256)}, u32[]{:S(2)}) copy-start(f32[256]{0:T(256)} %param.31) | copy-start | bytes 3076
  (1 other events, 0.6 us)
Sparse Core Ops, SparseCore 0:
  9.5 43.6 all-gather.4
  55.5 47.5 all-gather.2
